TPU v7x, 128 devices: a whole 4x4x4 slice. The times are simulated.
128 devices in a mesh: ctx: 8 (over z, core), tp: 8 (over y_lo, x), grp: 2 (over y_hi).
Axes of the slice: x: 4, y: 4 (y_hi: 2, y_lo: 2; y = y_hi * 2 + y_lo), z: 4, core: 2. Of those that a mesh axis runs over, the one named last changes fastest.
Arguments:
- merged_hidden: bfloat16 [8192, 5120], P(('ctx', 'grp')), may hold values from -40 to 40
- counts: int32 [16], replicated, may hold values from 1 to 32, 192 in all
- owner: int32 [16, 32], replicated, may hold values from 0 to 15, as said below
- down_proj: bfloat16 [5120, 8192], P(None, 'tp'), may hold values from -0.078125 to 0.078125
- text_embed: bfloat16 [8192, 8192], P(('ctx', 'grp'), 'tp'), may hold values from -64 to 64
- norm_gain: float32 [8192], replicated, may hold values from 0.1 to 1.9
- w_query: bfloat16 [8192, 4096], P(None, 'tp')
- w_key: bfloat16 [8192, 1024], P(None, 'tp')
- w_value: bfloat16 [8192, 1024], P(None, 'tp'), may hold values from -0.0625 to 0.0625
Outputs:
- attended: bfloat16 [8192, 4096], P(('ctx', 'grp'), 'tp')
Inputs may be any that keep to these rules, and one draw needn't show every extreme that they name: `owner`: for each encoder device, window slot i goes to shard p[i mod (8 * 2)] for a permutation p of the shards drawn for that device, so one device's live windows reach one shard at most 2 times. `counts`: the live windows of all devices number 192.
All inputs are finite; a program needn't handle non-finite values.
Results may differ from a plain program's by a relative error of at most 0.013.
The roundings to bfloat16 on the way count: a program that leaves them out, or rounds other values in their place, can miss the bound.
Values may be sent and summed in bfloat16 or wider, within the bound.
A program may use at most 256 MiB of HBM per device.

v0:
```python
import jax
import jax.numpy as jnp
from jax import lax
from jax.sharding import PartitionSpec as P

HD = 128


def route_tables(counts, owner, holders, wcap):
    slot_ids = jnp.arange(wcap, dtype=jnp.int32)
    live = slot_ids[None, :] < counts[:, None]
    shards = jnp.arange(holders, dtype=jnp.int32)
    hits = ((owner[:, :, None] == shards[None, None, :]) & live[:, :, None]).astype(jnp.int32)
    per_pair = jnp.sum(hits, axis=1, dtype=jnp.int32)
    before = jnp.cumsum(per_pair, axis=0, dtype=jnp.int32) - per_pair
    earlier = jnp.cumsum(hits, axis=1, dtype=jnp.int32) - hits
    rank = jnp.sum(earlier * hits, axis=2, dtype=jnp.int32)
    return (live, per_pair, before, rank)


def attend(queries, q_pos, keys, values, head_dim):
    rows = queries.shape[0]
    kv_heads = keys.shape[1] // head_dim
    q_heads = queries.shape[1] // head_dim
    group = q_heads // kv_heads
    q_grid = queries.reshape(rows, kv_heads, group, head_dim)
    last_query = jnp.max(q_pos)
    init = (
        jnp.full((kv_heads, group, rows), -1e30, jnp.float32),
        jnp.zeros((kv_heads, group, rows), jnp.float32),
        jnp.zeros((kv_heads, group, rows, head_dim), jnp.float32),
    )
    pieces = (
        lax.all_gather(keys, ("ctx", "grp"), axis=0, tiled=True),
        lax.all_gather(values, ("ctx", "grp"), axis=0, tiled=True),
    )

    def update(state):
        top, total, accum = state
        key_piece, value_piece = pieces
        count = key_piece.shape[0]
        k_grid = key_piece.reshape(count, kv_heads, head_dim)
        v_grid = value_piece.reshape(count, kv_heads, head_dim)
        scores = jnp.einsum(
            "rkgd,nkd->kgrn", q_grid, k_grid, preferred_element_type=jnp.float32
        ) * head_dim ** (-0.5)
        k_pos = jnp.arange(count, dtype=jnp.int32)
        allowed = k_pos[None, :] <= q_pos[:, None]
        scores = jnp.where(allowed, scores, -1e30)
        new_top = jnp.maximum(top, jnp.max(scores, axis=3))
        weights = jnp.where(allowed, jnp.exp(scores - new_top[..., None]), 0.0)
        new_total = jnp.sum(weights, axis=3)
        added = jnp.einsum(
            "kgrn,nkd->kgrd",
            weights.astype(jnp.bfloat16),
            v_grid,
            preferred_element_type=jnp.float32,
        )
        return (new_top, new_total, added)

    top, total, accum = lax.cond(jnp.int32(0) <= last_query, update, lambda state: state, init)
    result = accum / total[..., None]
    return result.transpose(2, 0, 1, 3).reshape(rows, q_heads * head_dim).astype(jnp.bfloat16)


def local(merged_hidden, counts, owner, down_proj, text_embed, norm_gain, w_query, w_key, w_value):
    holders = lax.axis_size(("ctx", "grp"))
    device = lax.axis_index(("ctx", "grp"))
    wcap = owner.shape[1]
    rows_dev = text_embed.shape[0]
    window = rows_dev // wcap
    most = wcap // holders
    windows_dev = rows_dev // window
    live, per_pair, before, rank = route_tables(counts, owner, holders, wcap)
    image = jnp.dot(merged_hidden, down_proj, preferred_element_type=jnp.float32).astype(
        jnp.bfloat16
    )
    my_live = lax.dynamic_index_in_dim(live, device, 0, False)
    my_owner = lax.dynamic_index_in_dim(owner, device, 0, False)
    my_rank = lax.dynamic_index_in_dim(rank, device, 0, False)
    slot_of = my_owner * most + my_rank
    slot_ids = jnp.arange(holders * most, dtype=jnp.int32)
    select = ((slot_of[None, :] == slot_ids[:, None]) & my_live[None, :]).astype(jnp.bfloat16)
    arrivals = lax.dynamic_index_in_dim(per_pair, device, 1, False)
    offsets = lax.dynamic_index_in_dim(before, device, 1, False)
    slot_rank = jnp.arange(most, dtype=jnp.int32)
    dest = (offsets[:, None] + slot_rank[None, :]).reshape(-1)
    valid = (slot_rank[None, :] < arrivals[:, None]).reshape(-1)
    window_ids = jnp.arange(windows_dev, dtype=jnp.int32)
    place = ((dest[None, :] == window_ids[:, None]) & valid[None, :]).astype(jnp.bfloat16)
    filled = jnp.sum(arrivals)
    image_mask = jnp.arange(rows_dev, dtype=jnp.int32) // window < filled
    width = image.shape[1]
    grid = image.reshape(wcap, window, width)
    packed = jnp.einsum("aw,wtc->atc", select, grid, preferred_element_type=jnp.float32).astype(
        jnp.bfloat16
    )
    arrived = lax.all_to_all(
        packed.reshape(holders, most * window, width),
        ("ctx", "grp"),
        split_axis=0,
        concat_axis=0,
        tiled=True,
    )
    width = arrived.shape[-1]
    grid = arrived.reshape(holders * most, window, width)
    placed = jnp.einsum("pa,atc->ptc", place, grid, preferred_element_type=jnp.float32).astype(
        jnp.bfloat16
    )
    own_cols = jnp.where(image_mask[:, None], placed.reshape(rows_dev, width), text_embed)
    sequence = lax.all_gather(own_cols, "tp", axis=1, tiled=True)
    values32 = sequence.astype(jnp.float32)
    scale = lax.rsqrt(jnp.mean(values32 * values32, axis=1, keepdims=True) + 1e-06)
    normed = (values32 * scale * norm_gain[None, :]).astype(jnp.bfloat16)
    queries = jnp.dot(normed, w_query, preferred_element_type=jnp.float32).astype(jnp.bfloat16)
    keys = jnp.dot(normed, w_key, preferred_element_type=jnp.float32).astype(jnp.bfloat16)
    values = jnp.dot(normed, w_value, preferred_element_type=jnp.float32).astype(jnp.bfloat16)
    own_pos = device * rows_dev + jnp.arange(rows_dev, dtype=jnp.int32)
    attended = attend(queries, own_pos, keys, values, HD)
    return attended


def solution(mesh):
    in_specs = (
        P(("ctx", "grp"), None),
        P(),
        P(),
        P(None, "tp"),
        P(("ctx", "grp"), "tp"),
        P(),
        P(None, "tp"),
        P(None, "tp"),
        P(None, "tp"),
    )
    out_specs = P(("ctx", "grp"), "tp")
    return jax.shard_map(local, mesh=mesh, in_specs=in_specs, out_specs=out_specs, check_vma=False)
```

profile of v0, /device:TPU:96, one launch (start us, length us, event | category | flops | bytes accessed | tf_op | source)
XLA Modules:
  0.0 338.8 jit_solution(7701526052944786464)
XLA Ops:
  6.5 0.0 copy-start
  6.5 0.9 iota_compare_fusion.5
  7.4 0.1 copy.38
  7.5 0.8 copy.37
  8.3 1.0 fusion.51
  9.3 0.2 add_reduce_fusion
  9.5 9.8 %convolution_convert_fusion = bf16[512,1024]{1,0:T(8,128)(2,1)S(1)} fusion(bf16[512,5120]{1,0:T(8,128)(2,1)} %param.11, bf16[5120,1024]{1,0:T(8,128)(2,1)} %param.14), kind=kOutput, calls=%fused_computation.24 | convolution fusion | flops 5369233408 | bytes 16777216 | tf_op jit(solution)/shard_map/dot_general | solution.py:75
  19.4 0.0 copy-start.1
  19.4 1.5 convolution_convert_fusion.2
  20.8 1.6 copy.41
  22.4 7.2 %all-to-all-start = ((bf16[16,32,1024]{2,1,0:T(8,128)(2,1)}), bf16[16,32,1024]{2,1,0:T(8,128)(2,1)S(1)}, u32[]{:S(2)}, u32[]{:S(2)}) async-start(bf16[16,32,1024]{2,1,0:T(8,128)(2,1)} %bitcast.11), calls=%async_computation | async-start | bytes 2097152 | tf_op jit(solution)/shard_map/all_to_all | solution.py:98
  29.6 0.0 all-gather.4.cloned.1.call-start
  29.6 0.2 convert_reduce_fusion
  29.9 0.7 dynamic-slice_reduce_fusion.1
  30.6 0.1 iota_compare_fusion.4
  30.7 0.1 lt.66
  30.8 0.1 iota_add_fusion
  30.8 0.1 add.71
  30.9 0.7 fusion.43
  31.6 13.4 %all-to-all-done = bf16[16,32,1024]{2,1,0:T(8,128)(2,1)S(1)} async-done(((bf16[16,32,1024]{2,1,0:T(8,128)(2,1)}), bf16[16,32,1024]{2,1,0:T(8,128)(2,1)S(1)}, u32[]{:S(2)}, u32[]{:S(2)}) %all-to-all-start) | async-done | bytes 1048608 | tf_op jit(solution)/shard_map/all_to_all | solution.py:98
  45.0 1.5 convolution_convert_fusion.1
  46.5 0.6 copy.43
  47.0 2.5 bitcast_select_fusion.1
  49.5 0.0 all-gather.4.cloned.1.call-update
  49.5 0.0 all-gather.6.cloned.1.call-start
  49.6 91.0 %all-gather.4.cloned.1.call-done = bf16[512,8192]{1,0:T(8,128)(2,1)} async-done(((bf16[512,1024]{1,0:T(8,128)(2,1)}), bf16[512,8192]{1,0:T(8,128)(2,1)}) %all-gather.4.cloned.1.call-update) | async-done | bytes 8388624 | tf_op jit(solution)/shard_map/all_gather | solution.py:111
  140.6 5.1 %fusion.20 = f32[512]{0:T(512)S(1)} fusion(bf16[512,8192]{1,0:T(8,128)(2,1)} %all-gather.4.cloned.1.call-done), kind=kLoop, calls=%fused_computation.21 | loop fusion | flops 12582400 | bytes 8390656 | tf_op jit(solution)/shard_map/reduce_sum | solution.py:113
  145.7 0.0 copy-done
  145.7 0.0 copy-done.1
  145.7 6.4 %convolution_convert_fusion.5 = bf16[512,128]{1,0:T(8,128)(2,1)} fusion(bf16[8192,128]{1,0:T(8,128)(2,1)S(1)} %copy-done, bf16[512,8192]{1,0:T(8,128)(2,1)} %all-gather.4.cloned.1.call-done, f32[8192]{0:T(1024)S(1)} %copy-done.1, f32[512]{0:T(512)S(1)} %add_rsqrt_fusion), kind=kOutput, calls=%fused_computation.31 | convolution fusion | flops 1090584576 | bytes 10651648 | tf_op jit(solution)/shard_map/dot_general | solution.py:116
  152.2 0.0 all-gather.6.cloned.1.call-update
  152.2 0.2 all-gather.8.cloned.1.call-start
  152.4 7.0 %convolution_convert_fusion.4 = bf16[512,128]{1,0:T(8,128)(2,1)} fusion(bf16[8192,128]{1,0:T(8,128)(2,1)} %param.19, bf16[512,8192]{1,0:T(8,128)(2,1)} %all-gather.4.cloned.1.call-done, f32[8192]{0:T(1024)S(1)} %copy-done.1, f32[512]{0:T(512)S(1)} %add_rsqrt_fusion), kind=kOutput, calls=%fused_computation.30 | convolution fusion | flops 1090584576 | bytes 10651648 | tf_op jit(solution)/shard_map/dot_general | solution.py:117
  159.4 0.0 all-gather.8.cloned.1.call-update
  159.5 0.6 fusion.47
  160.8 11.2 %convolution_convert_fusion.3 = bf16[512,512]{1,0:T(8,128)(2,1)} fusion(bf16[8192,512]{1,0:T(8,128)(2,1)} %param.17, bf16[512,8192]{1,0:T(8,128)(2,1)} %all-gather.4.cloned.1.call-done, f32[8192]{0:T(1024)S(1)} %copy-done.1, f32[512]{0:T(512)S(1)} %add_rsqrt_fusion), kind=kOutput, calls=%fused_computation.27 | convolution fusion | flops 4312006656 | bytes 17336320 | tf_op jit(solution)/shard_map/dot_general | solution.py:115
  171.9 26.4 %all-gather.6.cloned.1.call-done = bf16[8192,128]{1,0:T(8,128)(2,1)} async-done(((bf16[512,128]{1,0:T(8,128)(2,1)}), bf16[8192,128]{1,0:T(8,128)(2,1)}) %all-gather.6.cloned.1.call-update) | async-done | bytes 2097168 | tf_op jit(solution)/shard_map/all_gather | solution.py:34
  198.4 48.9 %all-gather.8.cloned.1.call-done = bf16[8192,128]{1,0:T(8,128)(2,1)} async-done(((bf16[512,128]{1,0:T(8,128)(2,1)}), bf16[8192,128]{1,0:T(8,128)(2,1)}) %all-gather.8.cloned.1.call-update) | async-done | bytes 2097168 | tf_op jit(solution)/shard_map/all_gather | solution.py:35
  247.2 83.4 %conditional.1 = (f32[1,4,512]{2,1,0:T(4,128)S(1)}, f32[1,4,512,128]{3,2,1,0:T(8,128)S(1)}) conditional(s32[]{:T(128)} %convert_element_type.44, () %tuple.13, (s32[512]{0:T(512)S(1)}, bf16[512,512]{1,0:T(8,128)(2,1)}, bf16[8192,128]{1,0:T(8,128)(2,1)}, bf16[8192,128]{1,0:T(8,128)(2,1)}) %tuple.14), branch_computations={%region_7.8_spmd, %region_8.11_spmd} | conditional | flops 8812230656 | bytes 223922192 | solution.py:61
  247.2 5.5 %iota_compare_fusion = pred[512,8192]{0,1:T(8,128)(4,1)} fusion(s32[512]{0:T(512)S(1)} %get-tuple-element.14), kind=kLoop, calls=%fused_computation.8 | loop fusion | flops 4194304 | bytes 4196352 | tf_op jit(solution)/shard_map/cond/branch_1_fun/le | solution.py:48
  252.7 27.3 %fusion = (f32[4,512]{1,0:T(4,128)S(1)}, f32[8192,512,4]{1,0,2:T(8,128)}) fusion(pred[512,8192]{0,1:T(8,128)(4,1)} %iota_compare_fusion, bf16[8192,128]{1,0:T(8,128)(2,1)} %get-tuple-element.15, bf16[512,512]{1,0:T(8,128)(2,1)} %get-tuple-element.16), kind=kOutput, calls=%fused_computation.2 | convolution fusion | flops 4345296896 | bytes 73932800 | tf_op jit(solution)/shard_map/cond/branch_1_fun/rkgd,nkd->kgrn/dot_general | solution.py:44
  280.0 27.7 %fusion.10 = f32[1,4,512,128]{3,2,1,0:T(8,128)S(1)} fusion(bf16[8192,128]{1,0:T(8,128)(2,1)} %get-tuple-element.17, f32[8192,512,4]{1,0,2:T(8,128)} %get-tuple-element.26, f32[4,512]{1,0:T(4,128)S(1)} %broadcast_maximum_fusion, pred[512,8192]{0,1:T(8,128)(4,1)} %iota_compare_fusion), kind=kOutput, calls=%fused_computation.12 | convolution fusion | flops 4378853376 | bytes 74457088 | tf_op jit(solution)/shard_map/cond/branch_1_fun/kgrn,nkd->kgrd/dot_general | solution.py:53
  307.7 22.9 %fusion.2 = f32[4,512]{1,0:T(4,128)S(1)} fusion(f32[8192,512,4]{1,0,2:T(8,128)} %get-tuple-element.26, f32[4,512]{1,0:T(4,128)S(1)} %broadcast_maximum_fusion, pred[512,8192]{0,1:T(8,128)(4,1)} %iota_compare_fusion), kind=kLoop, calls=%fused_computation.4 | loop fusion | flops 83884032 | bytes 71319552 | tf_op jit(solution)/shard_map/cond/branch_1_fun/reduce_sum | solution.py:52
  330.6 0.3 fusion.26
  331.0 0.4 copy.44
  331.4 0.9 copy.59
  (5 shorter events, 0.1 us)
Async XLA Ops:
  6.5 139.2 %copy-start = (bf16[8192,128]{1,0:T(8,128)(2,1)S(1)}, bf16[8192,128]{1,0:T(8,128)(2,1)}, u32[]{:S(2)}) copy-start(bf16[8192,128]{1,0:T(8,128)(2,1)} %param.18) | copy-start | bytes 6291460
  19.4 126.4 %copy-start.1 = (f32[8192]{0:T(1024)S(1)}, f32[8192]{0:T(1024)}, u32[]{:S(2)}) copy-start(f32[8192]{0:T(1024)} %param.16) | copy-start | bytes 98308
  22.4 22.6 %all-to-all-start = ((bf16[16,32,1024]{2,1,0:T(8,128)(2,1)}), bf16[16,32,1024]{2,1,0:T(8,128)(2,1)S(1)}, u32[]{:S(2)}, u32[]{:S(2)}) async-start(bf16[16,32,1024]{2,1,0:T(8,128)(2,1)} %bitcast.11), calls=%async_computation | async-start | bytes 2097152 | tf_op jit(solution)/shard_map/all_to_all | solution.py:98
  29.6 111.0 %all-gather.4.cloned.1.call-start = ((), (), s32[]{:S(2)}) async-start(), calls=%async_computation.1 | async-start | bytes 9437184 | tf_op jit(solution)/shard_map/all_gather | solution.py:111
  49.5 148.8 %all-gather.6.cloned.1.call-start = ((), (), s32[]{:S(2)}) async-start(), calls=%async_computation.2 | async-start | bytes 2228224 | tf_op jit(solution)/shard_map/all_gather | solution.py:34
  152.2 95.0 %all-gather.8.cloned.1.call-start = ((), (), s32[]{:S(2)}) async-start(), calls=%async_computation.3 | async-start | bytes 2228224 | tf_op jit(solution)/shard_map/all_gather | solution.py:35
Sparse Core Ops, SparseCore 0:
  49.7 90.9 all-gather.3
  152.3 45.9 all-gather.5
  200.8 46.3 all-gather.7
where the time goes:
time: 342 us; the launch traced here: 339 us
  waiting for transfers between devices  180 us (53%)
  matrix products  92.4 us (27%)
  other arithmetic  40.8 us (12%)
  between operations  13.9 us (4%)
  starting transfers between devices  7.46 us (2%)
  local copies, waits for them, and re-layouts  4.51 us (1%)
    all_gather x1, waiting for transfers between devices, local(): sequence = lax.all_gather(own_cols, 'tp', axis=1, tiled=True)  91 us
    all_gather x1, waiting for transfers between devices, attend(): lax.all_gather(values, ('ctx', 'grp'), axis=0, tiled=True)  48.9 us
    dot_general x1, matrix products, update(): jnp.einsum('kgrn,nkd->kgrd', weights.astype(jnp.bfloat16), v_grid, prefer...  27.7 us
    dot_general x1, matrix products, update(): jnp.einsum('rkgd,nkd->kgrn', q_grid, k_grid, preferred_element_type=jnp.f...  27.3 us
    all_gather x1, waiting for transfers between devices, attend(): lax.all_gather(keys, ('ctx', 'grp'), axis=0, tiled=True)  26.4 us
    reduce_sum x1, other arithmetic, update(): new_total = jnp.sum(weights, axis=3)  22.9 us
    all_to_all x1, waiting for transfers between devices, local(): lax.all_to_all(packed.reshape(holders, most * window, width), ('ctx', 'gr...  13.4 us
    dot_general x1, matrix products, local(): jnp.dot(normed, w_query, preferred_element_type=jnp.float32)  11.2 us
  transfers between devices with their start and end apart: 4, of which 4 were waited for; matrix products, arithmetic and copies ran while one was open for 6% of the time, Pallas kernels for 0%

commit v1 on v0

v1 whole, which is shorter than its diff:
```python
import functools
import math

import jax
import jax.numpy as jnp
from jax import lax
from jax.experimental import pallas as pl
from jax.experimental.pallas import tpu as pltpu
from jax.sharding import PartitionSpec as P

HD = 128
NC = 4
MESH = pl.DeviceIdType.MESH
NEG = float("-inf")


def route_tables(counts, owner, holders, wcap):
    slot_ids = jnp.arange(wcap, dtype=jnp.int32)
    live = slot_ids[None, :] < counts[:, None]
    shards = jnp.arange(holders, dtype=jnp.int32)
    hits = ((owner[:, :, None] == shards[None, None, :]) & live[:, :, None]).astype(jnp.int32)
    per_pair = jnp.sum(hits, axis=1, dtype=jnp.int32)
    before = jnp.cumsum(per_pair, axis=0, dtype=jnp.int32) - per_pair
    earlier = jnp.cumsum(hits, axis=1, dtype=jnp.int32) - hits
    rank = jnp.sum(earlier * hits, axis=2, dtype=jnp.int32)
    return (live, per_pair, before, rank)


def layer_kernel(
    own_in, gain, wq_in, wk_in, wv_in, out,
    seq, wq, wkv, q, kv, m, l, acc, acc_q, acc_kv,
    ld_sem, w_sem, gs, gr, ks, kr, fs, fr,
):
    rows, cols = own_in.shape
    chunk = rows // NC
    half = chunk // 2
    heads = q.shape[0]
    ctx = lax.axis_index("ctx")
    tp = lax.axis_index("tp")
    yh = lax.axis_index("grp")
    z, core = lax.div(ctx, 2), lax.rem(ctx, 2)
    yl, x = lax.div(tp, 4), lax.rem(tp, 4)
    rank = ctx * 2 + yh

    def at(dx, dy):
        return lax.rem(yl + dy, 2) * 4 + lax.rem(x + dx, 4)

    to_xp, to_xm, to_yp = {"tp": at(1, 0)}, {"tp": at(3, 0)}, {"tp": at(0, 1)}
    sibling = {"ctx": z * 2 + 1 - core}

    def mate(dz, dy):
        return {
            "ctx": lax.rem(z + dz, 4) * 2 + core,
            "grp": lax.rem(yh + dy, 2),
        }

    own_load = []
    for i in range(NC):
        r = pl.ds(i * chunk, chunk)
        own_load.append(
            pltpu.make_async_copy(own_in.at[r], seq.at[0, r], ld_sem.at[i])
        )
        own_load[i].start()
    w_load = [
        pltpu.make_async_copy(wk_in, wkv.at[:, :, pl.ds(0, HD)], w_sem.at[0]),
        pltpu.make_async_copy(wv_in, wkv.at[:, :, pl.ds(HD, HD)], w_sem.at[1]),
        pltpu.make_async_copy(wq_in, wq, w_sem.at[2]),
    ]
    for c in w_load:
        c.start()

    barrier = pltpu.get_barrier_semaphore()
    partners = [to_xp, to_xm, to_yp, sibling]
    for n in range(1, 8):
        partners.append(mate(n // 2, n % 2))
    for dev in partners:
        pl.semaphore_signal(barrier, inc=1, device_id=dev, device_id_type=MESH)
    pl.semaphore_wait(barrier, len(partners))

    def remote(src, dst, ssem, rsem, dev):
        return pltpu.make_async_remote_copy(
            src_ref=src, dst_ref=dst, send_sem=ssem, recv_sem=rsem,
            device_id=dev, device_id_type=MESH,
        )

    moves = {}

    def send(i, name, src_slot, dst_slot, r, dev, index):
        c = remote(
            seq.at[src_slot, r], seq.at[dst_slot, r], gs.at[i, index], gr.at[i, index], dev
        )
        c.start()
        moves[i, name] = c

    def whole(i):
        return pl.ds(i * chunk, chunk)

    def first(i):
        own_load[i].wait()
        send(i, "own_y", 0, 3, whole(i), to_yp, 0)
        send(i, "own_xp", 0, 1, whole(i), to_xp, 1)
        send(i, "own_xm", 0, 2, whole(i), to_xm, 2)

    def second(i):
        moves[i, "own_xp"].wait_recv()
        send(i, "opp_a", 1, 6, pl.ds(i * chunk, half), to_xp, 3)
        moves[i, "own_xm"].wait_recv()
        send(i, "opp_b", 2, 6, pl.ds(i * chunk + half, half), to_xm, 4)
        moves[i, "own_y"].wait_recv()
        send(i, "mate_xp", 3, 4, whole(i), to_xp, 5)
        send(i, "mate_xm", 3, 5, whole(i), to_xm, 6)

    def third(i):
        moves[i, "opp_a"].wait_recv()
        moves[i, "opp_b"].wait_recv()
        send(i, "opp_y", 6, 7, whole(i), to_yp, 7)

    places = [(0, 0), (3, 0), (1, 0), (0, 1), (3, 1), (1, 1), (2, 0), (2, 1)]
    kv_moves = {}

    def project(i):
        r = whole(i)
        for name in ("mate_xp", "mate_xm", "opp_y"):
            moves[i, name].wait_recv()
        total = jnp.zeros((chunk, 1), jnp.float32)
        for k in range(8):
            v = seq[k, r].astype(jnp.float32)
            total = total + jnp.sum(v * v, axis=1, keepdims=True)
        scale = lax.rsqrt(total / (8 * cols) + 1e-06)
        for k in range(8):
            b = at(*places[k])
            v = seq[k, r].astype(jnp.float32)
            normed = (v * scale * gain[pl.ds(b, 1), :]).astype(jnp.bfloat16)
            part_kv = jnp.dot(normed, wkv[b], preferred_element_type=jnp.float32)
            part_q = jnp.dot(normed, wq[b], preferred_element_type=jnp.float32)
            if k == 0:
                acc_kv[...] = part_kv
                acc_q[...] = part_q
            else:
                acc_kv[...] += part_kv
                acc_q[...] += part_q
        kv[0, 0, r] = acc_kv[...].astype(jnp.bfloat16)
        for h in range(heads):
            q[h, r] = acc_q[:, h * HD:(h + 1) * HD].astype(jnp.bfloat16)
        for n in range(1, 8):
            c = remote(
                kv.at[0, 0, r], kv.at[n, 0, r], ks.at[n, i], kr.at[n, i], mate(n // 2, n % 2)
            )
            kv_moves[n, i] = c
            if n == 1:
                c.start()
            else:
                @pl.when(z + n // 2 <= 3)
                def _():
                    c.start()

    first(0)
    first(1)
    for c in w_load:
        c.wait()
    for i in range(NC + 2):
        if i < NC:
            second(i)
        if i + 2 < NC:
            first(i + 2)
        if 0 <= i - 1 < NC:
            third(i - 1)
        if 0 <= i - 2 < NC:
            project(i - 2)

    m[...] = jnp.full(m.shape, NEG, jnp.float32)
    l[...] = jnp.zeros(l.shape, jnp.float32)
    acc[...] = jnp.zeros(acc.shape, jnp.float32)
    scale2 = math.log2(math.e) / math.sqrt(HD)

    def attend(n, c, masked):
        tile = min(256, rows)
        for h in range(heads):
            for t in range(rows // tile):
                r = pl.ds(t * tile, tile)
                s = lax.dot_general(
                    q[h, r], kv[n, c, :, :HD], (((1,), (1,)), ((), ())),
                    preferred_element_type=jnp.float32,
                )
                if masked:
                    qi = lax.broadcasted_iota(jnp.int32, s.shape, 0) + t * tile
                    ki = lax.broadcasted_iota(jnp.int32, s.shape, 1)
                    s = jnp.where(ki <= qi, s, NEG)
                old = m[h, r]
                new = jnp.maximum(old, jnp.max(s, axis=1, keepdims=True))
                m[h, r] = new
                fade = jnp.exp2((old - new) * scale2)
                p = jnp.exp2((s - new[:, :1]) * scale2)
                part = p[:, :128]
                for j in range(1, rows // 128):
                    part = part + p[:, j * 128:(j + 1) * 128]
                l[h, r] = l[h, r] * fade + part
                acc[h, r] = acc[h, r] * fade + jnp.dot(
                    p.astype(jnp.bfloat16), kv[n, c, :, HD:],
                    preferred_element_type=jnp.float32,
                )

    def forward(n):
        return remote(kv.at[n, 0], kv.at[n, 1], fs.at[n], fr.at[n], sibling)

    forward(0).start()
    attend(0, 0, True)

    @pl.loop(1, 8)
    def _(n):
        dz, dy = lax.div(n, 2), lax.rem(n, 2)

        @pl.when(z - dz >= 0)
        def _():
            for i in range(NC):
                r = whole(i)
                remote(
                    kv.at[0, 0, r], kv.at[n, 0, r], ks.at[n, i], kr.at[n, i], sibling
                ).wait_recv()
            forward(n).start()

        src = (z - dz) * 4 + core * 2 + lax.rem(yh + dy, 2)

        @pl.when(jnp.logical_and(z - dz >= 0, src < rank))
        def _():
            attend(n, 0, False)

    @pl.loop(0, 8)
    def _(n):
        dz, dy = lax.div(n, 2), lax.rem(n, 2)

        @pl.when(z - dz >= 0)
        def _():
            forward(n).wait_recv()

        src = (z - dz) * 4 + (1 - core) * 2 + lax.rem(yh + dy, 2)

        @pl.when(jnp.logical_and(z - dz >= 0, src < rank))
        def _():
            attend(n, 1, False)

    for h in range(heads):
        total = jnp.sum(l[h], axis=1, keepdims=True)
        out[:, h * HD:(h + 1) * HD] = (acc[h] / total).astype(jnp.bfloat16)

    for c in moves.values():
        c.wait_send()
    for (n, i), c in kv_moves.items():
        if n == 1:
            c.wait_send()
        else:
            @pl.when(z + n // 2 <= 3)
            def _():
                c.wait_send()

    @pl.loop(0, 8)
    def _(n):
        @pl.when(z - lax.div(n, 2) >= 0)
        def _():
            forward(n).wait_send()


def layer(own_cols, norm_gain, w_query, w_key, w_value):
    rows, cols = own_cols.shape
    blocks = norm_gain.shape[0] // cols
    q_cols = w_query.shape[1]
    heads = q_cols // HD
    any_space = pl.BlockSpec(memory_space=pl.ANY)
    vmem = pl.BlockSpec(memory_space=pltpu.VMEM)
    dma = pltpu.SemaphoreType.DMA
    return pl.pallas_call(
        layer_kernel,
        out_shape=jax.ShapeDtypeStruct((rows, q_cols), jnp.bfloat16),
        in_specs=[any_space, vmem, any_space, any_space, any_space],
        out_specs=vmem,
        scratch_shapes=[
            pltpu.VMEM((8, rows, cols), jnp.bfloat16),
            pltpu.VMEM((blocks, cols, q_cols), jnp.bfloat16),
            pltpu.VMEM((blocks, cols, 2 * HD), jnp.bfloat16),
            pltpu.VMEM((heads, rows, HD), jnp.bfloat16),
            pltpu.VMEM((8, 2, rows, 2 * HD), jnp.bfloat16),
            pltpu.VMEM((heads, rows, 128), jnp.float32),
            pltpu.VMEM((heads, rows, 128), jnp.float32),
            pltpu.VMEM((heads, rows, HD), jnp.float32),
            pltpu.VMEM((rows // NC, q_cols), jnp.float32),
            pltpu.VMEM((rows // NC, 2 * HD), jnp.float32),
            dma((NC,)),
            dma((3,)),
            dma((NC, 8)),
            dma((NC, 8)),
            dma((8, NC)),
            dma((8, NC)),
            dma((8,)),
            dma((8,)),
        ],
        compiler_params=pltpu.CompilerParams(
            collective_id=0, has_side_effects=True, vmem_limit_bytes=60 * 1024 * 1024
        ),
        name="layer",
    )(
        own_cols,
        norm_gain.reshape(blocks, cols),
        w_query.reshape(blocks, cols, q_cols),
        w_key.reshape(blocks, cols, HD),
        w_value.reshape(blocks, cols, HD),
    )


def local(merged_hidden, counts, owner, down_proj, text_embed, norm_gain, w_query, w_key, w_value):
    holders = lax.axis_size(("ctx", "grp"))
    device = lax.axis_index(("ctx", "grp"))
    wcap = owner.shape[1]
    rows_dev = text_embed.shape[0]
    window = rows_dev // wcap
    most = wcap // holders
    windows_dev = rows_dev // window
    live, per_pair, before, rank = route_tables(counts, owner, holders, wcap)
    image = jnp.dot(merged_hidden, down_proj, preferred_element_type=jnp.float32).astype(
        jnp.bfloat16
    )
    my_live = lax.dynamic_index_in_dim(live, device, 0, False)
    my_owner = lax.dynamic_index_in_dim(owner, device, 0, False)
    my_rank = lax.dynamic_index_in_dim(rank, device, 0, False)
    slot_of = my_owner * most + my_rank
    slot_ids = jnp.arange(holders * most, dtype=jnp.int32)
    select = ((slot_of[None, :] == slot_ids[:, None]) & my_live[None, :]).astype(jnp.bfloat16)
    arrivals = lax.dynamic_index_in_dim(per_pair, device, 1, False)
    offsets = lax.dynamic_index_in_dim(before, device, 1, False)
    slot_rank = jnp.arange(most, dtype=jnp.int32)
    dest = (offsets[:, None] + slot_rank[None, :]).reshape(-1)
    valid = (slot_rank[None, :] < arrivals[:, None]).reshape(-1)
    window_ids = jnp.arange(windows_dev, dtype=jnp.int32)
    place = ((dest[None, :] == window_ids[:, None]) & valid[None, :]).astype(jnp.bfloat16)
    filled = jnp.sum(arrivals)
    image_mask = jnp.arange(rows_dev, dtype=jnp.int32) // window < filled
    width = image.shape[1]
    grid = image.reshape(wcap, window, width)
    packed = jnp.einsum("aw,wtc->atc", select, grid, preferred_element_type=jnp.float32).astype(
        jnp.bfloat16
    )
    arrived = lax.all_to_all(
        packed.reshape(holders, most * window, width),
        ("ctx", "grp"),
        split_axis=0,
        concat_axis=0,
        tiled=True,
    )
    width = arrived.shape[-1]
    grid = arrived.reshape(holders * most, window, width)
    placed = jnp.einsum("pa,atc->ptc", place, grid, preferred_element_type=jnp.float32).astype(
        jnp.bfloat16
    )
    own_cols = jnp.where(image_mask[:, None], placed.reshape(rows_dev, width), text_embed)
    return layer(own_cols, norm_gain, w_query, w_key, w_value)


def solution(mesh):
    in_specs = (
        P(("ctx", "grp"), None),
        P(),
        P(),
        P(None, "tp"),
        P(("ctx", "grp"), "tp"),
        P(),
        P(None, "tp"),
        P(None, "tp"),
        P(None, "tp"),
    )
    out_specs = P(("ctx", "grp"), "tp")
    return jax.shard_map(local, mesh=mesh, in_specs=in_specs, out_specs=out_specs, check_vma=False)
```

time: 342 us -> 171 us (0.50)
  the two profiles are of different devices: /device:TPU:96 before, /device:TPU:121 now
where the time goes in v1:
time: 171 us
  Pallas kernels  130 us (76%)
  matrix products  12.8 us (7%)
  waiting for transfers between devices  10 us (6%)
  starting transfers between devices  7.25 us (4%)
  local copies, waits for them, and re-layouts  5.72 us (3%)
  other arithmetic  5.13 us (3%)
    pallas_call x1, Pallas kernels, layer(): pl.pallas_call(layer_kernel, out_shape=jax.ShapeDtypeStruct((rows, q_cols...  130 us
    all_to_all x1, waiting for transfers between devices, local(): lax.all_to_all(packed.reshape(holders, most * window, width), ('ctx', 'gr...  10 us
    dot_general x1, matrix products, local(): jnp.dot(merged_hidden, down_proj, preferred_element_type=jnp.float32)  9.83 us
    all_to_all x1, starting transfers between devices, local(): lax.all_to_all(packed.reshape(holders, most * window, width), ('ctx', 'gr...  7.25 us
  transfers between devices with their start and end apart: 1, of which 1 were waited for; matrix products, arithmetic and copies ran while one was open for 2% of the time, Pallas kernels for 0%

profile of v1, /device:TPU:121, one launch (start us, length us, event | category | flops | bytes accessed | tf_op | source)
XLA Modules:
  0.0 170.6 jit_solution(3864472118368852953)
XLA Ops:
  0.0 0.8 copy.27
  0.8 0.7 iota_compare_fusion.4
  1.5 0.1 copy.28
  1.6 1.0 fusion.23
  2.6 0.2 add_reduce_fusion
  2.8 9.8 %convolution_convert_fusion = bf16[512,1024]{1,0:T(8,128)(2,1)S(1)} fusion(bf16[512,5120]{1,0:T(8,128)(2,1)} %param.9, bf16[5120,1024]{1,0:T(8,128)(2,1)} %param.12), kind=kOutput, calls=%fused_computation | convolution fusion | flops 5369233408 | bytes 16777216 | tf_op jit(solution)/shard_map/dot_general | solution.py:318
  12.7 0.0 copy-start.1
  12.7 0.0 copy-start
  12.7 1.5 convolution_convert_fusion.2
  14.2 1.6 copy.31
  15.7 7.2 %all-to-all-start = ((bf16[16,32,1024]{2,1,0:T(8,128)(2,1)}), bf16[16,32,1024]{2,1,0:T(8,128)(2,1)S(1)}, u32[]{:S(2)}, u32[]{:S(2)}) async-start(bf16[16,32,1024]{2,1,0:T(8,128)(2,1)} %bitcast.4), calls=%async_computation | async-start | bytes 2097152 | tf_op jit(solution)/shard_map/all_to_all | solution.py:341
  23.0 0.2 convert_reduce_fusion
  23.2 0.8 dynamic-slice_reduce_fusion.1
  24.0 0.1 iota_add_fusion
  24.1 0.1 add.52
  24.2 0.1 iota_compare_fusion.3
  24.3 0.1 lt.66
  24.4 0.0 copy-done.1
  24.4 0.6 reshape.92.gain
  25.0 0.7 fusion.19
  25.7 10.0 %all-to-all-done = bf16[16,32,1024]{2,1,0:T(8,128)(2,1)S(1)} async-done(((bf16[16,32,1024]{2,1,0:T(8,128)(2,1)}), bf16[16,32,1024]{2,1,0:T(8,128)(2,1)S(1)}, u32[]{:S(2)}, u32[]{:S(2)}) %all-to-all-start) | async-done | bytes 1048608 | tf_op jit(solution)/shard_map/all_to_all | solution.py:341
  35.7 1.5 convolution_convert_fusion.1
  37.2 0.6 copy.33
  37.8 0.0 copy-done
  37.8 1.3 bitcast_select_fusion.own_in
  39.1 129.7 %layer.1 = bf16[512,512]{1,0:T(8,128)(2,1)} custom-call(bf16[512,1024]{1,0:T(8,128)(2,1)} %bitcast_select_fusion.own_in, f32[8,1024]{1,0:T(8,128)} %reshape.92.gain, bf16[8,1024,512]{2,1,0:T(8,128)(2,1)} %bitcast.18, bf16[8,1024,128]{2,1,0:T(8,128)(2,1)} %bitcast.20, bf16[8,1024,128]{2,1,0:T(8,128)(2,1)} %bitcast.21), custom_call_target="tpu_custom_call" | custom-call | tf_op jit(solution)/shard_map/layer/pallas_call | solution.py:271
  168.8 1.9 %copy.39 = bf16[512,512]{1,0:T(8,128)(2,1)} copy(bf16[512,512]{1,0:T(8,128)(2,1)} %layer.1) | data formatting | bytes 1048576
  (2 shorter events, 0.0 us)
Async XLA Ops:
  12.7 11.7 %copy-start.1 = (f32[8192]{0:T(1024)S(1)}, f32[8192]{0:T(1024)}, u32[]{:S(2)}) copy-start(f32[8192]{0:T(1024)} %param.14) | copy-start | bytes 98308
  12.7 25.1 %copy-start = (bf16[512,1024]{1,0:T(8,128)(2,1)S(1)}, bf16[512,1024]{1,0:T(8,128)(2,1)}, u32[]{:S(2)}) copy-start(bf16[512,1024]{1,0:T(8,128)(2,1)} %param.13) | copy-start | bytes 3145732
  15.7 20.0 %all-to-all-start = ((bf16[16,32,1024]{2,1,0:T(8,128)(2,1)}), bf16[16,32,1024]{2,1,0:T(8,128)(2,1)S(1)}, u32[]{:S(2)}, u32[]{:S(2)}) async-start(bf16[16,32,1024]{2,1,0:T(8,128)(2,1)} %bitcast.4), calls=%async_computation | async-start | bytes 2097152 | tf_op jit(solution)/shard_map/all_to_all | solution.py:341
